TPU v7x, 256 devices: a whole 4x4x8 slice. The times are simulated.
256 devices in a mesh: rows: 64 (over z, x, core), samp: 4 (over y).
Axes of the slice: x: 4, y: 4, z: 8, core: 2. Of those that a mesh axis runs over, the one named last changes fastest.
Arguments:
- samples: bfloat16 [2, 32768, 2048], P(None, None, ('rows', 'samp')), may hold values from -6 to 6
- factor: bfloat16 [2, 32768, 4096], P(None, ('rows', 'samp')), as said below
- diag_inverse: bfloat16 [2, 32768, 512], P(None, 'rows'), as said below
Outputs:
- solved: float32 [2, 32768, 2048], P(None, None, ('rows', 'samp'))
Inputs may be any that keep to these rules, and one draw needn't show every extreme that they name: `factor`: zero on and above the diagonal blocks: entries of rows of block b in panel k vanish unless b > k. `diag_inverse`: lower triangular within each block, diagonal between 0.5 and 1.
All inputs are finite; a program needn't handle non-finite values.
Results may differ from a plain program's by a relative error of at most 0.0065.
Values may be sent and summed in bfloat16 or wider, within the bound.
A program may use at most 128 MiB of HBM per device.

v0:
```python
import jax
import jax.numpy as jnp
from jax import lax
from jax.sharding import PartitionSpec as P


def broadcast(block, axis, source):
    block = jnp.where(lax.axis_index(axis) == source, block, jnp.zeros_like(block))
    return lax.psum(block, axis)


def local(samples, factor, diag_inverse):
    row_count = lax.axis_size("rows")
    my_position = lax.axis_index("rows")
    regrouped = lax.all_to_all(samples, "rows", split_axis=1, concat_axis=2, tiled=True)
    working = regrouped.astype(jnp.float32)
    blocks_here = working.shape[0]
    block_rows = diag_inverse.shape[2]
    panel_count = factor.shape[2] // block_rows
    block_index = jnp.arange(blocks_here) * row_count + my_position
    for panel_index in range(panel_count):
        owner_index = panel_index % row_count
        local_slot = panel_index // row_count
        is_owner = my_position == owner_index
        current = working[local_slot]
        inverse_block = diag_inverse[local_slot]

        def solve_block(operands):
            return jnp.dot(
                operands[0].astype(jnp.float32), operands[1], precision=lax.Precision.HIGHEST
            )

        def empty_block(operands):
            return jnp.zeros_like(operands[1])

        solution = lax.cond(is_owner, solve_block, empty_block, (inverse_block, current))
        rounded = solution.astype(jnp.bfloat16)
        received = broadcast(rounded, "rows", owner_index)
        working = working.at[local_slot].set(jnp.where(is_owner, solution, current))
        lower_part = factor[:, :, panel_index * block_rows : (panel_index + 1) * block_rows]
        update = jnp.einsum(
            "jik,kc->jic",
            lax.all_gather(lower_part, "samp", axis=1, tiled=True),
            received,
            preferred_element_type=jnp.float32,
        )
        later = (block_index > panel_index)[:, None, None]
        working = jnp.where(later, working - update, working)
    return lax.all_to_all(working, "rows", split_axis=2, concat_axis=1, tiled=True)


def solution(mesh):
    placed = (
        P(None, None, ("rows", "samp")),
        P(None, ("rows", "samp"), None),
        P(None, "rows", None),
    )
    return jax.shard_map(
        local,
        mesh=mesh,
        in_specs=placed,
        out_specs=P(None, None, ("rows", "samp")),
        check_vma=False,
    )
```

profile of v0, /device:TPU:1, one launch (start us, length us, event | category | flops | bytes accessed | tf_op | source)
XLA Modules:
  0.0 1695.7 jit_solution(8756102841690367848)
XLA Ops:
  7.4 30.1 %copy.28 = bf16[2,32768,8]{2,0,1:T(2,128)(2,1)} copy(bf16[2,32768,8]{1,2,0:T(8,128)(2,1)} %param.35) | data formatting | bytes 2097152 | tf_op args[0]
  37.5 20.7 %reshape.285 = bf16[64,2,4096]{2,1,0:T(2,128)(2,1)} reshape(bf16[32768,2,8]{2,1,0:T(2,128)(2,1)} %bitcast.112) | data formatting | bytes 2097152
  58.1 13.0 all-to-all-start
  71.2 2.9 fusion.8
  74.3 24.8 %all-to-all-done = bf16[64,2,4096]{2,1,0:T(2,128)(2,1)S(1)} async-done(((bf16[64,2,4096]{2,1,0:T(2,128)(2,1)}), bf16[64,2,4096]{2,1,0:T(2,128)(2,1)S(1)}, u32[]{:S(2)}, u32[]{:S(2)}) %all-to-all-start) | async-done | bytes 1048608 | tf_op jit(solution)/shard_map/all_to_all | solution.py:15
  99.1 20.8 %reshape.286 = bf16[32768,2,8]{2,1,0:T(2,128)(2,1)} reshape(bf16[64,2,4096]{2,1,0:T(2,128)(2,1)S(1)} %all-to-all-done) | data formatting | bytes 2097152
  119.9 31.8 %copy.29 = f32[2,64,512,8]{2,3,1,0:T(8,128)S(1)} copy(bf16[2,64,512,8]{3,0,2,1:T(2,128)(2,1)} %bitcast.111) | data formatting | bytes 3145728 | tf_op jit(solution)/shard_map/convert_element_type | solution.py:16
  152.0 1.0 copy-done.11
  153.0 0.9 convert_select_fusion.7
  153.9 0.7 all-gather.11.cloned.1.call-update
  154.7 1.3 copy.82
  156.6 1.2 bitcast_dynamic-update-slice_fusion.7
  157.8 173.0 %all-reduce.9.cloned.1.call-done = bf16[512,512]{0,1:T(8,128)(2,1)} async-done(((bf16[512,512]{0,1:T(8,128)(2,1)}), bf16[512,512]{0,1:T(8,128)(2,1)}) %all-reduce.9.cloned.1.call-update) | async-done | bytes 524304 | tf_op jit(solution)/shard_map/psum | solution.py:9
  330.7 2.8 subtract_select_fusion.7
  333.6 1.0 slice_bitcast_fusion.6
  334.6 3.2 conditional.9
  334.6 3.2 fusion.10
  337.8 2.1 convert_select_fusion.6
  340.0 0.7 all-gather.13.cloned.1.call-update
  340.8 1.4 bitcast_dynamic-update-slice_fusion.6
  342.2 174.4 %all-reduce.11.cloned.1.call-done = bf16[512,512]{0,1:T(8,128)(2,1)} async-done(((bf16[512,512]{0,1:T(8,128)(2,1)}), bf16[512,512]{0,1:T(8,128)(2,1)}) %all-reduce.11.cloned.1.call-update) | async-done | bytes 524304 | tf_op jit(solution)/shard_map/psum | solution.py:9
  516.6 2.1 subtract_select_fusion.6
  518.8 1.1 slice_bitcast_fusion.5
  520.6 1.0 copy-done.13
  521.5 0.9 convert_select_fusion.5
  523.1 1.4 bitcast_dynamic-update-slice_fusion.5
  524.6 176.7 %all-reduce.13.cloned.1.call-done = bf16[512,512]{0,1:T(8,128)(2,1)} async-done(((bf16[512,512]{0,1:T(8,128)(2,1)}), bf16[512,512]{0,1:T(8,128)(2,1)}) %all-reduce.13.cloned.1.call-update) | async-done | bytes 524304 | tf_op jit(solution)/shard_map/psum | solution.py:9
  701.3 2.1 subtract_select_fusion.5
  703.4 1.1 slice_bitcast_fusion.4
  705.2 1.0 copy-done.14
  706.2 0.9 convert_select_fusion.4
  707.9 1.4 bitcast_dynamic-update-slice_fusion.4
  709.4 176.5 %all-reduce.15.cloned.1.call-done = bf16[512,512]{0,1:T(8,128)(2,1)} async-done(((bf16[512,512]{0,1:T(8,128)(2,1)}), bf16[512,512]{0,1:T(8,128)(2,1)}) %all-reduce.15.cloned.1.call-update) | async-done | bytes 524304 | tf_op jit(solution)/shard_map/psum | solution.py:9
  885.9 2.1 subtract_select_fusion.4
  888.0 1.1 slice_bitcast_fusion.3
  889.8 1.0 copy-done.15
  890.8 0.9 convert_select_fusion.3
  892.3 1.4 bitcast_dynamic-update-slice_fusion.3
  893.8 177.3 %all-reduce.17.cloned.1.call-done = bf16[512,512]{0,1:T(8,128)(2,1)} async-done(((bf16[512,512]{0,1:T(8,128)(2,1)}), bf16[512,512]{0,1:T(8,128)(2,1)}) %all-reduce.17.cloned.1.call-update) | async-done | bytes 524304 | tf_op jit(solution)/shard_map/psum | solution.py:9
  1071.1 2.1 subtract_select_fusion.3
  1073.3 1.1 slice_bitcast_fusion.2
  1075.1 1.0 copy-done.16
  1076.1 0.9 convert_select_fusion.2
  1077.0 0.7 all-gather.21.cloned.1.call-update
  1077.8 1.4 bitcast_dynamic-update-slice_fusion.2
  1079.3 1.3 copy-done.8
  1080.5 175.2 %all-reduce.19.cloned.1.call-done = bf16[512,512]{0,1:T(8,128)(2,1)} async-done(((bf16[512,512]{0,1:T(8,128)(2,1)}), bf16[512,512]{0,1:T(8,128)(2,1)}) %all-reduce.19.cloned.1.call-update) | async-done | bytes 524304 | tf_op jit(solution)/shard_map/psum | solution.py:9
  1255.8 2.8 subtract_select_fusion.2
  1258.6 1.0 slice_bitcast_fusion.1
  1259.8 1.0 copy-done.17
  1260.7 0.9 convert_select_fusion.1
  1261.7 0.7 all-gather.23.cloned.1.call-update
  1262.5 1.4 bitcast_dynamic-update-slice_fusion.1
  1263.9 176.5 %all-reduce.21.cloned.1.call-done = bf16[512,512]{0,1:T(8,128)(2,1)} async-done(((bf16[512,512]{0,1:T(8,128)(2,1)}), bf16[512,512]{0,1:T(8,128)(2,1)}) %all-reduce.21.cloned.1.call-update) | async-done | bytes 524304 | tf_op jit(solution)/shard_map/psum | solution.py:9
  1440.5 2.1 subtract_select_fusion.1
  1442.6 1.1 slice_bitcast_fusion
  1444.4 1.0 copy-done.18
  1445.4 0.9 convert_select_fusion
  1446.4 1.4 bitcast_dynamic-update-slice_fusion
  1447.8 177.0 %all-reduce.23.cloned.1.call-done = bf16[512,512]{0,1:T(8,128)(2,1)} async-done(((bf16[512,512]{0,1:T(8,128)(2,1)}), bf16[512,512]{0,1:T(8,128)(2,1)}) %all-reduce.23.cloned.1.call-update) | async-done | bytes 524304 | tf_op jit(solution)/shard_map/psum | solution.py:9
  1624.8 2.1 subtract_select_fusion
  1627.0 1.6 copy.54
  1628.6 58.0 %all_to_all.27 = f32[2,512,512]{1,0,2:T(2,128)S(1)} all-to-all(f32[2,512,512]{1,0,2:T(2,128)S(1)} %copy.54), channel_id=1, replica_groups=mesh['rows'=64,'samp'=4] {'rows'}, dimensions={2} | all-to-all | bytes 4194304 | tf_op jit(solution)/shard_map/all_to_all | solution.py:49
  1686.6 1.7 copy.55
  (92 shorter events, 8.1 us)
Async XLA Ops:
  58.1 41.0 %all-to-all-start = ((bf16[64,2,4096]{2,1,0:T(2,128)(2,1)}), bf16[64,2,4096]{2,1,0:T(2,128)(2,1)S(1)}, u32[]{:S(2)}, u32[]{:S(2)}) async-start(bf16[64,2,4096]{2,1,0:T(2,128)(2,1)} %reshape.285), calls=%async_computation | async-start | bytes 2097152 | tf_op jit(solution)/shard_map/all_to_all | solution.py:15
  71.1 3.1 copy-start.19
  71.1 86.7 %all-gather.9.cloned.1.call-start = ((), (), s32[]{:S(2)}) async-start(), calls=%async_computation.3 | async-start | bytes 1310720 | tf_op jit(solution)/shard_map/all_gather | solution.py:43
  74.1 256.6 %all-reduce.9.cloned.1.call-start = ((), (), s32[]{:S(2)}) async-start(), calls=%async_computation.2 | async-start | bytes 1048576 | tf_op jit(solution)/shard_map/psum | solution.py:9
  152.0 1.0 copy-start.11
  153.8 188.4 %all-gather.11.cloned.1.call-start = ((), (), s32[]{:S(2)}) async-start(), calls=%async_computation.5 | async-start | bytes 1310720 | tf_op jit(solution)/shard_map/all_gather | solution.py:43
  154.6 362.0 %all-reduce.11.cloned.1.call-start = ((), (), s32[]{:S(2)}) async-start(), calls=%async_computation.4 | async-start | bytes 1048576 | tf_op jit(solution)/shard_map/psum | solution.py:9
  154.7 1.9 copy-start.12
  339.9 184.6 %all-gather.13.cloned.1.call-start = ((), (), s32[]{:S(2)}) async-start(), calls=%async_computation.7 | async-start | bytes 1310720 | tf_op jit(solution)/shard_map/all_gather | solution.py:43
  340.7 360.6 %all-reduce.13.cloned.1.call-start = ((), (), s32[]{:S(2)}) async-start(), calls=%async_computation.6 | async-start | bytes 1048576 | tf_op jit(solution)/shard_map/psum | solution.py:9
  518.8 1.7 copy-start
  520.6 1.0 copy-start.13
  520.6 2.5 copy-start.1
  522.4 187.0 %all-gather.15.cloned.1.call-start = ((), (), s32[]{:S(2)}) async-start(), calls=%async_computation.9 | async-start | bytes 1310720 | tf_op jit(solution)/shard_map/all_gather | solution.py:43
  523.0 362.9 %all-reduce.15.cloned.1.call-start = ((), (), s32[]{:S(2)}) async-start(), calls=%async_computation.8 | async-start | bytes 1048576 | tf_op jit(solution)/shard_map/psum | solution.py:9
  703.4 1.7 copy-start.2
  705.2 1.0 copy-start.14
  705.2 2.7 copy-start.3
  707.1 186.8 %all-gather.17.cloned.1.call-start = ((), (), s32[]{:S(2)}) async-start(), calls=%async_computation.11 | async-start | bytes 1310720 | tf_op jit(solution)/shard_map/all_gather | solution.py:43
  707.6 363.5 %all-reduce.17.cloned.1.call-start = ((), (), s32[]{:S(2)}) async-start(), calls=%async_computation.10 | async-start | bytes 1048576 | tf_op jit(solution)/shard_map/psum | solution.py:9
  888.0 1.7 copy-start.4
  889.8 1.0 copy-start.15
  889.8 2.5 copy-start.5
  891.7 187.6 %all-gather.19.cloned.1.call-start = ((), (), s32[]{:S(2)}) async-start(), calls=%async_computation.13 | async-start | bytes 1310720 | tf_op jit(solution)/shard_map/all_gather | solution.py:43
  892.3 363.5 %all-reduce.19.cloned.1.call-start = ((), (), s32[]{:S(2)}) async-start(), calls=%async_computation.12 | async-start | bytes 1048576 | tf_op jit(solution)/shard_map/psum | solution.py:9
  1073.3 1.7 copy-start.6
  1075.1 1.0 copy-start.16
  1075.1 2.7 copy-start.7
  1076.9 187.0 %all-gather.21.cloned.1.call-start = ((), (), s32[]{:S(2)}) async-start(), calls=%async_computation.15 | async-start | bytes 1310720 | tf_op jit(solution)/shard_map/all_gather | solution.py:43
  1077.7 362.8 %all-reduce.21.cloned.1.call-start = ((), (), s32[]{:S(2)}) async-start(), calls=%async_computation.14 | async-start | bytes 1048576 | tf_op jit(solution)/shard_map/psum | solution.py:9
  1079.2 1.3 copy-start.8
  1259.7 1.0 copy-start.17
  1261.6 186.2 %all-gather.23.cloned.1.call-start = ((), (), s32[]{:S(2)}) async-start(), calls=%async_computation.17 | async-start | bytes 1310720 | tf_op jit(solution)/shard_map/all_gather | solution.py:43
  1262.4 362.5 %all-reduce.23.cloned.1.call-start = ((), (), s32[]{:S(2)}) async-start(), calls=%async_computation.16 | async-start | bytes 1048576 | tf_op jit(solution)/shard_map/psum | solution.py:9
  1442.6 1.7 copy-start.9
  1444.4 1.0 copy-start.18
  1444.4 2.0 copy-start.10
Sparse Core Ops, SparseCore 0:
  74.3 26.7 all-gather.8
  156.5 22.9 all-gather.10
  342.6 22.6 all-gather.12
  524.8 24.8 all-gather.14
  709.4 24.8 all-gather.16
  894.0 25.4 all-gather.18
  1079.6 24.8 all-gather.20
  1264.3 24.8 all-gather.22
Sparse Core Ops, SparseCore 1:
  153.9 176.8 all-reduce.8
  340.0 176.5 all-reduce.10
  522.5 178.7 all-reduce.12
  707.1 178.7 all-reduce.14
  891.8 179.3 all-reduce.16
  1077.0 178.7 all-reduce.18
  1261.7 178.7 all-reduce.20
  1446.4 178.4 all-reduce.22
where the time goes:
time: 1700 us
  waiting for transfers between devices  1440 us (85%)
  local copies, waits for them, and re-layouts  131 us (8%)
  blocking collectives  58 us (3%)
  matrix products  21.6 us (1%)
  other arithmetic  19.5 us (1%)
    psum x8, waiting for transfers between devices, broadcast(): return lax.psum(block, axis)  1410 us
    unnamed x44, local copies, waits for them, and re-layouts  84.3 us
    all_to_all x1, blocking collectives, local(): lax.all_to_all(working, 'rows', split_axis=2, concat_axis=1, tiled=True)  58 us
  transfers between devices with their start and end apart: 17, of which 9 were waited for; matrix products, arithmetic and copies ran while one was open for 6% of the time, Pallas kernels for 0%

commit v1 on v0

v1 whole, which is shorter than its diff:
```python
import functools

import jax
import jax.numpy as jnp
from jax import lax
from jax.experimental import pallas as pl
from jax.experimental.pallas import tpu as pltpu
from jax.sharding import PartitionSpec as P

MESH = pl.DeviceIdType.MESH
X_CHIPS = 4
CHUNKS = 4


def dot_nt(left, right):
    return lax.dot_general(
        left, right, (((1,), (1,)), ((), ())), preferred_element_type=jnp.float32
    )


def solve_kernel(
    n_rows, n_samp, panels, sample_ref, factor_ref, inverse_ref, out_ref,
    gathered, solved, working, inverse, factor_sem, solved_sem, send_factor, send_solved, local_sem,
):
    block = inverse.shape[0]
    columns = working.shape[1]
    chunk = columns // CHUNKS
    part = block // n_samp
    plane = 2 * X_CHIPS
    z_chips = n_rows // plane
    me, samp = lax.axis_index("rows"), lax.axis_index("samp")
    z, x, core = me // plane, (me // 2) % X_CHIPS, me % 2

    def at(z_to, x_to, core_to):
        return (z_to * X_CHIPS + x_to) * 2 + core_to

    right = at(z, (x + 1) % X_CHIPS, core)
    left = at(z, (x + X_CHIPS - 1) % X_CHIPS, core)
    above = at((z + 1) % z_chips, x, core)
    below = at((z + z_chips - 1) % z_chips, x, core)
    mate = at(z, x, 1 - core)

    barrier = pltpu.get_barrier_semaphore()
    greeted = [right, left, above, mate] + ([below] if z_chips > 2 else [])
    for other in greeted:
        pl.semaphore_signal(barrier, inc=1, device_id=(other, samp), device_id_type=MESH)
    for step in range(1, n_samp):
        pl.semaphore_signal(
            barrier, inc=1, device_id=(me, (samp + step) % n_samp), device_id_type=MESH
        )
    pl.semaphore_wait(barrier, len(greeted) + n_samp - 1)

    def gather(index, carry):
        slot, panel = index // panels, index % panels
        source = factor_ref.at[slot, :, pl.ds(pl.multiple_of(panel * block, block), block)]
        target = gathered.at[slot, panel, pl.ds(pl.multiple_of(samp * part, part), part), :]
        for step in range(1, n_samp):
            pltpu.make_async_remote_copy(
                src_ref=source, dst_ref=target, send_sem=send_factor, recv_sem=factor_sem.at[slot, panel],
                device_id=(me, (samp + step) % n_samp), device_id_type=MESH,
            ).start()
        pltpu.make_async_copy(source, target, factor_sem.at[slot, panel]).start()
        return carry

    lax.fori_loop(0, 2 * panels, gather, 0)

    in_chain = me < plane

    @pl.when(in_chain)
    def _():
        copy = pltpu.make_async_copy(inverse_ref.at[0], inverse, local_sem)
        copy.start()
        copy.wait()

    for slot in range(2):
        working[slot] = sample_ref[:, slot].astype(jnp.float32).reshape(columns, block)

    def wait_factor(slot, panel):
        whole = gathered.at[slot, panel]
        pltpu.make_async_copy(whole, whole, factor_sem.at[slot, panel]).wait()

    def item(index, carry):
        key = index // 2
        piece = key % 2 + 2 * (index % 2)
        panel = (key - piece + CHUNKS) // 2 - CHUNKS // 2
        rows = pl.ds(pl.multiple_of(piece * chunk, chunk), chunk)

        @pl.when((panel >= 0) & (panel < panels))
        def _():
            place = pl.ds(pl.multiple_of(panel * columns + piece * chunk, chunk), chunk)
            block_ref = solved.at[place]

            @pl.when(me == panel)
            def _():
                value = working[0, rows, :]
                high = value.astype(jnp.bfloat16)
                rest = value - high.astype(jnp.float32)
                middle = rest.astype(jnp.bfloat16)
                low = (rest - middle.astype(jnp.float32)).astype(jnp.bfloat16)
                product = dot_nt(jnp.concatenate([high, middle, low], axis=0), inverse[...])
                answer = product[:chunk] + (product[chunk : 2 * chunk] + product[2 * chunk :])
                working[0, rows, :] = answer
                solved[place, :] = answer.astype(jnp.bfloat16)

            @pl.when(me != panel)
            def _():
                pltpu.make_async_copy(block_ref, block_ref, solved_sem.at[panel, piece]).wait()

            def send(condition, which, other):
                @pl.when(condition)
                def _():
                    pltpu.make_async_remote_copy(
                        src_ref=block_ref, dst_ref=block_ref, send_sem=send_solved.at[which],
                        recv_sem=solved_sem.at[panel, piece], device_id=(other, samp), device_id_type=MESH,
                    ).start()

            same = core == panel % 2
            away = (x + X_CHIPS - panel // 2) % X_CHIPS
            send(same, 0, mate)
            send(same & ((away == 0) | ((away == 1) & (piece % 2 == 0))), 1, right)
            send(same & ((away == 0) | ((away == X_CHIPS - 1) & (piece % 2 == 1))), 2, left)
            send(same & (away == 0) & (z < z_chips // 2), 3, above)
            if z_chips > 2:
                send(same & (away == 0) & ((z == 0) | (z > z_chips // 2 + 1)), 4, below)

            @pl.when(in_chain & (piece == 0))
            def _():
                wait_factor(0, panel)

            @pl.when(in_chain & (me > panel))
            def _():
                working[0, rows, :] -= dot_nt(solved[place, :], gathered[0, panel])

        return carry

    lax.fori_loop(0, 2 * (2 * panels + CHUNKS - 2), item, 0)

    def update(slot):
        def body(panel, carry):
            wait_factor(slot, panel)
            whole = pl.ds(pl.multiple_of(panel * columns, columns), columns)
            working[slot] -= dot_nt(solved[whole, :], gathered[slot, panel])
            return carry

        lax.fori_loop(0, panels, body, 0)

    @pl.when(jnp.logical_not(in_chain))
    def _():
        update(0)

    update(1)
    for slot in range(2):
        out_ref[:, slot] = working[slot].reshape(n_rows, columns // n_rows, block).astype(jnp.bfloat16)

    def wait_sent(ref, sem):
        pltpu.make_async_copy(ref, ref, sem).wait()

    wait_sent(gathered.at[:, pl.ds(0, panels * (n_samp - 1) // n_samp)], send_factor)
    wait_sent(solved.at[pl.ds(0, panels // 2 * columns)], send_solved.at[0])
    for which in (1, 2):
        wait_sent(solved.at[pl.ds(0, panels // plane * 6 * chunk)], send_solved.at[which])
    column = solved.at[pl.ds(0, panels // plane * columns)]

    @pl.when(z < z_chips // 2)
    def _():
        wait_sent(column, send_solved.at[3])

    if z_chips > 2:
        @pl.when((z == 0) | (z > z_chips // 2 + 1))
        def _():
            wait_sent(column, send_solved.at[4])


def local(samples, factor, diag_inverse):
    n_rows, n_samp = lax.axis_size("rows"), lax.axis_size("samp")
    slots, order, own = samples.shape
    block = diag_inverse.shape[2]
    panels = factor.shape[2] // block
    columns = own * n_rows
    turned = samples.transpose(0, 2, 1).reshape(slots, own, n_rows, block).transpose(2, 0, 1, 3)
    regrouped = lax.all_to_all(turned, "rows", split_axis=0, concat_axis=0, tiled=True)
    result = pl.pallas_call(
        functools.partial(solve_kernel, n_rows, n_samp, panels),
        out_shape=jax.ShapeDtypeStruct((n_rows, slots, own, block), jnp.bfloat16),
        in_specs=[
            pl.BlockSpec(memory_space=pltpu.VMEM),
            pl.BlockSpec(memory_space=pl.ANY),
            pl.BlockSpec(memory_space=pl.ANY),
        ],
        out_specs=pl.BlockSpec(memory_space=pltpu.VMEM),
        scratch_shapes=[
            pltpu.VMEM((slots, panels, block, block), jnp.bfloat16),
            pltpu.VMEM((panels * columns, block), jnp.bfloat16),
            pltpu.VMEM((slots, columns, block), jnp.float32),
            pltpu.VMEM((block, block), jnp.bfloat16),
            pltpu.SemaphoreType.DMA((slots, panels)),
            pltpu.SemaphoreType.DMA((panels, CHUNKS)),
            pltpu.SemaphoreType.DMA,
            pltpu.SemaphoreType.DMA((5,)),
            pltpu.SemaphoreType.DMA,
        ],
        compiler_params=pltpu.CompilerParams(
            collective_id=0, has_side_effects=True, vmem_limit_bytes=48 * 2**20
        ),
    )(regrouped, factor, diag_inverse)
    back = lax.all_to_all(result, "rows", split_axis=0, concat_axis=0, tiled=True)
    back = back.transpose(1, 2, 0, 3).reshape(slots, own, order)
    return back.astype(jnp.float32).transpose(0, 2, 1)


def solution(mesh):
    placed = (
        P(None, None, ("rows", "samp")),
        P(None, ("rows", "samp"), None),
        P(None, "rows", None),
    )
    return jax.shard_map(
        local,
        mesh=mesh,
        in_specs=placed,
        out_specs=P(None, None, ("rows", "samp")),
        check_vma=False,
    )
```

time: 1700 us -> 229 us (0.13)
  waiting for transfers between devices: 1440 us -> 0 us
  local copies, waits for them, and re-layouts: 131 us -> 3.03 us
  Pallas kernels: 0 us -> 124 us
  blocking collectives: 58 us -> 101 us
  matrix products: 21.6 us -> 0 us
  other arithmetic: 19.5 us -> 0.28 us
    psum x8 -> x0, waiting for transfers between devices: 1410 us -> none  [broadcast(): return lax.psum(block, axis)]
    pallas_call x0 -> x1, Pallas kernels: none -> 124 us  [local(): pl.pallas_call(functools.partial(solve_kernel, n_rows, n_samp, panels), o...]
    unnamed x44 -> x4, local copies, waits for them, and re-layouts: 84.3 us -> 0.01 us
    all_to_all x1 -> x2, blocking collectives: 58 us -> 101 us  [the longest x1 60.2 us: local(): lax.all_to_all(result, 'rows', split_axis=0, concat_axis=0, tiled=True)]
    convert_element_type x1 -> x0, local copies, waits for them, and re-layouts: 31.8 us -> none  [local(): working = regrouped.astype(jnp.float32)]
    all_to_all x1 -> x0, waiting for transfers between devices: 24.8 us -> none  [local(): lax.all_to_all(samples, 'rows', split_axis=1, concat_axis=2, tiled=True)]
    dot_general x8 -> x0, matrix products: 18.4 us -> none  [local(): jnp.einsum('jik,kc->jic', lax.all_gather(lower_part, 'samp', axis=1, tile...]
  transfers between devices with their start and end apart: 17 -> 0, of which waited for: 9 -> 0; matrix products, arithmetic and copies ran while one was open for 6% -> 0% of each run, Pallas kernels for 0% -> 0%
where the time goes in v1:
time: 229 us
  Pallas kernels  124 us (54%)
  blocking collectives  101 us (44%)
  local copies, waits for them, and re-layouts  3.03 us (1%)
    pallas_call x1, Pallas kernels, local(): pl.pallas_call(functools.partial(solve_kernel, n_rows, n_samp, panels), o...  124 us
    all_to_all x1, blocking collectives, local(): lax.all_to_all(result, 'rows', split_axis=0, concat_axis=0, tiled=True)  60.2 us
    all_to_all x1, blocking collectives, local(): lax.all_to_all(turned, 'rows', split_axis=0, concat_axis=0, tiled=True)  40.8 us

profile of v1, /device:TPU:1, one launch (start us, length us, event | category | flops | bytes accessed | tf_op | source)
XLA Modules:
  0.0 228.6 jit_solution(7415329618669372622)
XLA Ops:
  0.0 0.0 copy-start
  0.0 0.0 copy-start.1
  0.0 1.5 copy.9
  1.5 40.8 %all_to_all.10.sample_ref = bf16[64,2,8,512]{3,2,1,0:T(8,128)(2,1)S(1)} all-to-all(bf16[64,2,8,512]{3,2,1,0:T(8,128)(2,1)S(1)} %bitcast.14), channel_id=1, replica_groups=mesh['rows'=64,'samp'=4] {'rows'}, dimensions={0} | all-to-all | bytes 2097152 | tf_op jit(solution)/shard_map/all_to_all | solution.py:181
  42.3 0.0 copy-done
  42.3 0.0 copy-done.1
  42.3 124.3 %shard_map.37 = bf16[64,2,8,512]{3,2,1,0:T(8,128)(2,1)S(1)} custom-call(bf16[64,2,8,512]{3,2,1,0:T(8,128)(2,1)S(1)} %all_to_all.10.sample_ref, bf16[2,128,4096]{2,1,0:T(8,128)(2,1)S(1)} %copy-done, bf16[2,512,512]{2,1,0:T(8,128)(2,1)S(1)} %copy-done.1), custom_call_target="tpu_custom_call" | custom-call | tf_op jit(solution)/shard_map/pallas_call | solution.py:182
  166.6 60.2 %all_to_all.11 = bf16[64,2,8,512]{3,2,1,0:T(8,128)(2,1)S(1)} all-to-all(bf16[64,2,8,512]{3,2,1,0:T(8,128)(2,1)S(1)} %shard_map.37), channel_id=1, replica_groups=mesh['rows'=64,'samp'=4] {'rows'}, dimensions={0} | all-to-all | bytes 2097152 | tf_op jit(solution)/shard_map/all_to_all | solution.py:206
  226.8 0.3 convert_bitcast_fusion
  227.1 1.5 copy.7
Async XLA Ops:
  0.0 42.3 %copy-start = (bf16[2,128,4096]{2,1,0:T(8,128)(2,1)S(1)}, bf16[2,128,4096]{2,1,0:T(8,128)(2,1)}, u32[]{:S(2)}) copy-start(bf16[2,128,4096]{2,1,0:T(8,128)(2,1)} %factor_ref.1) | copy-start | bytes 6291460
  0.0 42.3 %copy-start.1 = (bf16[2,512,512]{2,1,0:T(8,128)(2,1)S(1)}, bf16[2,512,512]{2,1,0:T(8,128)(2,1)}, u32[]{:S(2)}) copy-start(bf16[2,512,512]{2,1,0:T(8,128)(2,1)} %inverse_ref.1) | copy-start | bytes 3145732

commit v2 on v1

v2 whole, which is shorter than its diff:
```python
import functools

import jax
import jax.numpy as jnp
from jax import lax
from jax.experimental import pallas as pl
from jax.experimental.pallas import tpu as pltpu
from jax.sharding import PartitionSpec as P

MESH = pl.DeviceIdType.MESH
X_CHIPS = 4
CHUNKS = X_CHIPS
SLOTS = 2


def dot_nt(left, right):
    return lax.dot_general(
        left, right, (((1,), (1,)), ((), ())), preferred_element_type=jnp.float32
    )


def wait_bytes(ref, sem):
    pltpu.make_async_copy(ref, ref, sem).wait()


def solve_kernel(
    n_rows, n_samp, panels, sample_ref, factor_ref, inverse_ref, out_ref,
    gathered, solved, working, inverse, arrived, leaving, landed,
    direct_sem, near_sem, far_sem, own_sem, solved_sem, sample_sem,
    sent_direct, sent_factor, sent_mate, sent_x, sent_z, sent_sample, sent_out, out_sem, inverse_sem,
):
    block = inverse.shape[0]
    columns = working.shape[1]
    chunk = columns // CHUNKS
    part = block // n_samp
    plane = 2 * X_CHIPS
    z_chips = n_rows // plane
    me, samp = lax.axis_index("rows"), lax.axis_index("samp")
    z, x, core = me // plane, (me // 2) % X_CHIPS, me % 2
    in_chain = z == 0

    def at(z_to, x_to, core_to):
        return (z_to * X_CHIPS + x_to) * 2 + core_to

    mate = at(z, x, 1 - core)

    def remote(source, target, send_sem, recv_sem, to_rows, to_samp):
        pltpu.make_async_remote_copy(
            src_ref=source, dst_ref=target, send_sem=send_sem, recv_sem=recv_sem,
            device_id=(to_rows, to_samp), device_id_type=MESH,
        ).start()

    barrier = pltpu.get_barrier_semaphore()

    def greet(step, carry):
        pl.semaphore_signal(
            barrier, inc=1, device_id=((me + step) % n_rows, samp), device_id_type=MESH
        )
        return carry

    lax.fori_loop(1, n_rows, greet, 0)
    for step in range(1, n_samp):
        pl.semaphore_signal(
            barrier, inc=1, device_id=(me, (samp + step) % n_samp), device_id_type=MESH
        )
    pl.semaphore_wait(barrier, n_rows + n_samp - 2)

    def rows_of(index):
        return pl.ds(pl.multiple_of(index * block, block), block)

    def send_sample(slot, to):
        source, target = sample_ref.at[slot, :, rows_of(to)], arrived.at[slot, me]

        @pl.when(to != me)
        def _():
            remote(source, target, sent_sample, sample_sem.at[slot], to, samp)

        @pl.when(to == me)
        def _():
            pltpu.make_async_copy(source, target, sample_sem.at[slot]).start()

    def send_window(to, carry):
        send_sample(0, to)
        return carry

    lax.fori_loop(0, plane, send_window, 0)

    def part_of(slot, panel, owner):
        return gathered.at[slot, panel, pl.ds(pl.multiple_of(owner * part, part), part), :]

    def own_part(slot, panel):
        return factor_ref.at[slot, :, rows_of(panel)]

    def send_direct(panel, carry):
        source, target = own_part(0, panel), part_of(0, panel, samp)
        pltpu.make_async_copy(source, target, direct_sem.at[panel]).start()
        for step in range(1, n_samp):
            remote(
                source, target, sent_direct.at[panel], direct_sem.at[panel],
                me, (samp + step) % n_samp,
            )
        return carry

    def send_near(slot):
        def body(panel, carry):
            source, target = own_part(slot, panel), part_of(slot, panel, samp)
            remote(source, target, sent_factor, near_sem.at[0, slot, panel], me, (samp + 1) % n_samp)
            remote(source, target, sent_factor, near_sem.at[1, slot, panel], me, (samp + 3) % n_samp)
            pltpu.make_async_copy(source, target, own_sem.at[slot, panel]).start()
            return carry

        lax.fori_loop(0, panels, body, 0)

    def relay(slot, panel):
        before, after = (samp + 3) % n_samp, (samp + 1) % n_samp
        from_before, from_after = part_of(slot, panel, before), part_of(slot, panel, after)
        wait_bytes(from_before, near_sem.at[0, slot, panel])
        wait_bytes(from_after, near_sem.at[1, slot, panel])

        @pl.when(panel % 2 == 0)
        def _():
            remote(from_before, from_before, sent_factor, far_sem.at[slot, panel], me, after)

        @pl.when(panel % 2 == 1)
        def _():
            remote(from_after, from_after, sent_factor, far_sem.at[slot, panel], me, before)

    def relays(slot, first, count):
        def body(step, carry):
            relay(slot, first + step)
            return carry

        lax.fori_loop(0, count, body, 0)

    def panel_rows(panel):
        return pl.ds(pl.multiple_of(panel * columns, columns), columns)

    def update(slot, panel):
        wait_bytes(part_of(slot, panel, (samp + 2) % n_samp), far_sem.at[slot, panel])
        wait_bytes(part_of(slot, panel, samp), own_sem.at[slot, panel])
        working[slot] -= dot_nt(solved[panel_rows(panel), :], gathered[slot, panel])

    def take_samples(slot):
        wait_bytes(arrived.at[slot], sample_sem.at[slot])
        working[slot] = arrived[slot].astype(jnp.float32).reshape(columns, block)

    def send_rows(slot):
        leaving[slot] = working[slot].reshape(n_rows, columns // n_rows, block).astype(jnp.bfloat16)
        target = landed.at[slot, :, rows_of(me)]
        pltpu.make_async_copy(leaving.at[slot, me], target, out_sem).start()

        def body(step, carry):
            to = (me + step) % n_rows
            remote(leaving.at[slot, to], target, sent_out, out_sem, to, samp)
            return carry

        lax.fori_loop(1, n_rows, body, 0)

    @pl.when(in_chain)
    def _():
        pltpu.make_async_copy(inverse_ref.at[0], inverse, inverse_sem).start()
        lax.fori_loop(0, me, send_direct, 0)
        send_near(1)

    @pl.when(jnp.logical_not(in_chain))
    def _():
        send_near(0)

    def send_rest(step, carry):
        send_sample(0, plane + (me + step) % (n_rows - plane))
        return carry

    lax.fori_loop(0, n_rows - plane, send_rest, 0)

    def send_second(step, carry):
        send_sample(1, (me + step) % n_rows)
        return carry

    lax.fori_loop(0, n_rows, send_second, 0)

    def place_of(panel, piece):
        return pl.ds(pl.multiple_of(panel * columns + piece * chunk, chunk), chunk)

    def holds(panel, piece_x):
        return (core == panel % 2) == (piece_x == panel // 2)

    def forward(panel, piece, sem, other):
        ref = solved.at[place_of(panel, piece)]
        remote(ref, ref, sem, solved_sem.at[panel, piece], other, samp)

    def receive(panel, piece):
        wait_bytes(solved.at[place_of(panel, piece)], solved_sem.at[panel, piece])

    def chain_item(index, carry):
        key = index // 2
        piece = key % 2 + 2 * (index % 2)
        panel = (key - piece + CHUNKS) // 2 - CHUNKS // 2
        rows = pl.ds(pl.multiple_of(piece * chunk, chunk), chunk)

        @pl.when((panel >= 0) & (panel < panels))
        def _():
            place = place_of(panel, piece)

            @pl.when(me == panel)
            def _():
                value = working[0, rows, :]
                high = value.astype(jnp.bfloat16)
                rest = value - high.astype(jnp.float32)
                middle = rest.astype(jnp.bfloat16)
                low = (rest - middle.astype(jnp.float32)).astype(jnp.bfloat16)
                product = dot_nt(jnp.concatenate([high, middle, low], axis=0), inverse[...])
                answer = product[:chunk] + (product[chunk : 2 * chunk] + product[2 * chunk :])
                working[0, rows, :] = answer
                solved[place, :] = answer.astype(jnp.bfloat16)

            @pl.when(me != panel)
            def _():
                receive(panel, piece)

            holder = holds(panel, x)

            @pl.when(holder)
            def _():
                forward(panel, piece, sent_mate, mate)

            @pl.when(me == panel)
            def _():
                for step in (1, 3, 2):
                    forward(panel, piece, sent_x, at(z, (x + step) % X_CHIPS, 1 - core))

            @pl.when(holder & (piece == x))
            def _():
                for z_to in ((2, 6) if z_chips == 8 else range(1, z_chips)):
                    forward(panel, piece, sent_z, at(z_to, x, core))

            @pl.when(me > panel)
            def _():
                @pl.when(piece == 0)
                def _():
                    wait_bytes(gathered.at[0, panel], direct_sem.at[panel])

                working[0, rows, :] -= dot_nt(solved[place, :], gathered[0, panel])

        return carry

    @pl.when(in_chain)
    def _():
        wait_bytes(inverse, inverse_sem)
        take_samples(0)
        lax.fori_loop(0, 2 * (2 * panels + CHUNKS - 2), chain_item, 0)
        send_rows(0)
        relays(1, 0, panels)

    def spread_item(step, carry):
        @pl.when(step < panels)
        def _():
            panel = step

            @pl.when(holds(panel, x))
            def _():
                receive(panel, x)
                if z_chips == 8:
                    @pl.when((z == 2) | (z == 6))
                    def _():
                        forward(panel, x, sent_z, at(z - 1, x, core))
                        forward(panel, x, sent_z, at(z + 1, x, core))

                        @pl.when((panel // 2) % 2 == z // 4)
                        def _():
                            forward(panel, x, sent_z, at(4, x, core))

                for hop in (2, 1, 3):
                    forward(panel, x, sent_x, at(z, (x + hop) % X_CHIPS, core))
                forward(panel, x, sent_mate, mate)

        @pl.when(step < panels // 2)
        def _():
            relays(0, 2 * step, 2)

        @pl.when(step == panels // 2)
        def _():
            send_near(1)

        @pl.when((step >= panels - 2) & (step < panels))
        def _():
            relays(1, 2 * (step - (panels - 2)), 2)

        @pl.when(step == 1)
        def _():
            take_samples(0)

        @pl.when(step >= 1)
        def _():
            panel = step - 1
            for hop in range(1, X_CHIPS):
                piece = (x + hop) % X_CHIPS

                @pl.when(holds(panel, piece))
                def _():
                    receive(panel, piece)
                    forward(panel, piece, sent_mate, mate)

            for hop in range(X_CHIPS):
                piece = (x + hop) % X_CHIPS

                @pl.when(jnp.logical_not(holds(panel, piece)))
                def _():
                    receive(panel, piece)

            update(0, panel)

        return carry

    @pl.when(jnp.logical_not(in_chain))
    def _():
        lax.fori_loop(0, panels + 1, spread_item, 0)
        send_rows(0)
        relays(1, 4, panels - 4)

    take_samples(1)

    def update_second(panel, carry):
        update(1, panel)
        return carry

    lax.fori_loop(0, panels, update_second, 0)
    send_rows(1)

    @pl.when(in_chain)
    def _():
        def sent(panel, carry):
            wait_bytes(gathered.at[0, 0, pl.ds(0, (n_samp - 1) * part), :], sent_direct.at[panel])
            return carry

        lax.fori_loop(0, me, sent, 0)
        wait_bytes(gathered.at[1, pl.ds(0, panels * 3 // n_samp)], sent_factor)
        copies = 4 * (2 if z_chips == 8 else z_chips - 1)
        wait_bytes(solved.at[pl.ds(0, copies * chunk)], sent_z)

    @pl.when(jnp.logical_not(in_chain))
    def _():
        wait_bytes(gathered.at[:, pl.ds(0, panels * 3 // n_samp)], sent_factor)

    if z_chips == 8:
        @pl.when((z == 2) | (z == 6))
        def _():
            wait_bytes(solved.at[pl.ds(0, 10 * chunk)], sent_z)

    wait_bytes(solved.at[pl.ds(0, 16 * chunk)], sent_mate)
    wait_bytes(solved.at[pl.ds(0, 12 * chunk)], sent_x)
    wait_bytes(arrived.at[:, pl.ds(0, n_rows - 1)], sent_sample)
    wait_bytes(leaving.at[:, pl.ds(0, n_rows - 1)], sent_out)
    wait_bytes(landed, out_sem)
    out_ref[...] = landed[...]


def local(samples, factor, diag_inverse):
    n_rows, n_samp = lax.axis_size("rows"), lax.axis_size("samp")
    slots, order, own = samples.shape
    block = diag_inverse.shape[2]
    panels = factor.shape[2] // block
    columns = own * n_rows
    result = pl.pallas_call(
        functools.partial(solve_kernel, n_rows, n_samp, panels),
        out_shape=jax.ShapeDtypeStruct((slots, own, order), jnp.bfloat16),
        in_specs=[pl.BlockSpec(memory_space=pl.ANY)] * 3,
        out_specs=pl.BlockSpec(memory_space=pltpu.VMEM),
        scratch_shapes=[
            pltpu.VMEM((slots, panels, block, block), jnp.bfloat16),
            pltpu.VMEM((panels * columns, block), jnp.bfloat16),
            pltpu.VMEM((slots, columns, block), jnp.float32),
            pltpu.VMEM((block, block), jnp.bfloat16),
            pltpu.VMEM((slots, n_rows, own, block), jnp.bfloat16),
            pltpu.VMEM((slots, n_rows, own, block), jnp.bfloat16),
            pltpu.VMEM((slots, own, order), jnp.bfloat16),
            pltpu.SemaphoreType.DMA((panels,)),
            pltpu.SemaphoreType.DMA((2, slots, panels)),
            pltpu.SemaphoreType.DMA((slots, panels)),
            pltpu.SemaphoreType.DMA((slots, panels)),
            pltpu.SemaphoreType.DMA((panels, CHUNKS)),
            pltpu.SemaphoreType.DMA((slots,)),
            pltpu.SemaphoreType.DMA((panels,)),
        ]
        + [pltpu.SemaphoreType.DMA] * 8,
        compiler_params=pltpu.CompilerParams(
            collective_id=0, has_side_effects=True, vmem_limit_bytes=60 * 2**20
        ),
    )(samples.transpose(0, 2, 1), factor, diag_inverse)
    return result.astype(jnp.float32).transpose(0, 2, 1)


def solution(mesh):
    placed = (
        P(None, None, ("rows", "samp")),
        P(None, ("rows", "samp"), None),
        P(None, "rows", None),
    )
    return jax.shard_map(
        local,
        mesh=mesh,
        in_specs=placed,
        out_specs=P(None, None, ("rows", "samp")),
        check_vma=False,
    )
```

time: 229 us -> 187 us (0.82)
  blocking collectives: 101 us -> 0 us
  Pallas kernels: 124 us -> 184 us
  local copies, waits for them, and re-layouts: 3.03 us -> 0 us
  other arithmetic: 0.28 us -> 2.68 us
    all_to_all x2 -> x0, blocking collectives: 101 us -> none  [the longest x1 60.2 us: local(): lax.all_to_all(result, 'rows', split_axis=0, concat_axis=0, tiled=True)]
    pallas_call x1, Pallas kernels: 124 us -> 184 us  [local(): pl.pallas_call(functools.partial(solve_kernel, n_rows, n_samp, panels), o...]
    transpose x0 -> x1, other arithmetic: none -> 2.68 us  [local(): return result.astype(jnp.float32).transpose(0, 2, 1)]
where the time goes in v2:
time: 187 us
  Pallas kernels  184 us (98%)
  other arithmetic  2.68 us (1%)
    pallas_call x1, Pallas kernels, local(): pl.pallas_call(functools.partial(solve_kernel, n_rows, n_samp, panels), o...  184 us

profile of v2, /device:TPU:1, one launch (start us, length us, event | category | flops | bytes accessed | tf_op | source)
XLA Modules:
  0.0 186.9 jit_solution(8475882065393493065)
XLA Ops:
  0.0 184.2 %shard_map.37 = bf16[2,8,32768]{2,1,0:T(8,128)(2,1)} custom-call(bf16[2,8,32768]{2,1,0:T(8,128)(2,1)} %bitcast.3, bf16[2,128,4096]{2,1,0:T(8,128)(2,1)} %factor_ref.1, bf16[2,512,512]{2,1,0:T(8,128)(2,1)} %inverse_ref.1), custom_call_target="tpu_custom_call" | custom-call | tf_op jit(solution)/shard_map/pallas_call | solution.py:363
  184.2 2.7 %convert_bitcast_fusion = f32[2,32768,8]{1,2,0:T(8,128)} fusion(bf16[2,8,32768]{2,1,0:T(8,128)(2,1)} %shard_map.37), kind=kLoop, calls=%fused_computation | loop fusion | flops 524288 | bytes 3145728 | tf_op jit(solution)/shard_map/transpose | solution.py:389

commit v3 on v2

--- a/solution.py
+++ b/solution.py
@@ -26,8 +26,9 @@
 def solve_kernel(
     n_rows, n_samp, panels, sample_ref, factor_ref, inverse_ref, out_ref,
     gathered, solved, working, inverse, arrived, leaving, landed,
-    direct_sem, near_sem, far_sem, own_sem, solved_sem, sample_sem,
-    sent_direct, sent_factor, sent_mate, sent_x, sent_z, sent_sample, sent_out, out_sem, inverse_sem,
+    direct_sem, near_sem, far_sem, own_sem, solved_sem, share_sem, sample_sem,
+    sent_direct, sent_factor, sent_mate, sent_chain, sent_share, sent_x, sent_z, sent_sample, sent_out, out_sem,
+    inverse_sem,
 ):
     block = inverse.shape[0]
     columns = working.shape[1]
@@ -35,6 +36,7 @@
     part = block // n_samp
     plane = 2 * X_CHIPS
     z_chips = n_rows // plane
+    share = chunk // z_chips
     me, samp = lax.axis_index("rows"), lax.axis_index("samp")
     z, x, core = me // plane, (me // 2) % X_CHIPS, me % 2
     in_chain = z == 0
@@ -181,12 +183,14 @@
     def place_of(panel, piece):
         return pl.ds(pl.multiple_of(panel * columns + piece * chunk, chunk), chunk)
 
-    def holds(panel, piece_x):
-        return (core == panel % 2) == (piece_x == panel // 2)
-
     def forward(panel, piece, sem, other):
         ref = solved.at[place_of(panel, piece)]
         remote(ref, ref, sem, solved_sem.at[panel, piece], other, samp)
+
+    def forward_share(panel, piece, index, send_sem, recv_sem, other):
+        start = panel * columns + piece * chunk + index * share
+        ref = solved.at[pl.ds(pl.multiple_of(start, share), share)]
+        remote(ref, ref, send_sem, recv_sem, other, samp)
 
     def receive(panel, piece):
         wait_bytes(solved.at[place_of(panel, piece)], solved_sem.at[panel, piece])
@@ -197,9 +201,10 @@
         panel = (key - piece + CHUNKS) // 2 - CHUNKS // 2
         rows = pl.ds(pl.multiple_of(piece * chunk, chunk), chunk)
 
-        @pl.when((panel >= 0) & (panel < panels))
+        @pl.when((panel >= 0) & (panel < 2 * x + 2))
         def _():
             place = place_of(panel, piece)
+            owner_x, owner_core = panel // 2, panel % 2
 
             @pl.when(me == panel)
             def _():
@@ -217,21 +222,39 @@
             def _():
                 receive(panel, piece)
 
-            holder = holds(panel, x)
-
-            @pl.when(holder)
+            @pl.when((me == panel) | ((core == 0) & (owner_x < x)))
             def _():
                 forward(panel, piece, sent_mate, mate)
 
+            @pl.when((me == panel) & (core == 1))
+            def _():
+                for ahead in (1, 3, 2):
+                    @pl.when(x + ahead < X_CHIPS)
+                    def _():
+                        forward(panel - 1, piece, sent_chain, at(z, x + ahead, 0))
+                        forward(panel, piece, sent_chain, at(z, x + ahead, 0))
+
             @pl.when(me == panel)
             def _():
-                for step in (1, 3, 2):
-                    forward(panel, piece, sent_x, at(z, (x + step) % X_CHIPS, 1 - core))
-
-            @pl.when(holder & (piece == x))
-            def _():
-                for z_to in ((2, 6) if z_chips == 8 else range(1, z_chips)):
-                    forward(panel, piece, sent_z, at(z_to, x, core))
+                for z_to in range(1, z_chips):
+                    forward_share(
+                        panel, piece, z_to, sent_share, share_sem.at[panel], at(z_to, piece, core)
+                    )
+
+                @pl.when(piece < x)
+                def _():
+                    forward_share(panel, piece, 0, sent_share, share_sem.at[panel], at(0, piece, core))
+
+            @pl.when((piece == x) & (core == owner_core))
+            def _():
+                for z_to in range(1, z_chips):
+                    forward_share(
+                        panel, piece, 0, sent_z, solved_sem.at[panel, piece], at(z_to, x, core)
+                    )
+                for x_to in range(X_CHIPS - 1):
+                    @pl.when(x_to < owner_x)
+                    def _():
+                        forward(panel, piece, sent_x, at(z, x_to, core))
 
             @pl.when(me > panel)
             def _():
@@ -243,78 +266,98 @@
 
         return carry
 
+    def spread_item(step, carry):
+        first = jnp.where(in_chain, 2 * x + 2, 0)
+
+        def with_panel(lag, body):
+            panel = step - lag
+
+            @pl.when((panel >= first) & (panel < panels))
+            def _():
+                body(panel, core == panel % 2, panel // 2)
+
+        def give_share(panel, mine, owner_x):
+            @pl.when(mine)
+            def _():
+                wait_bytes(solved.at[pl.ds(0, share)], share_sem.at[panel])
+                for hop in range(1, z_chips):
+                    z_to = (z + hop) % z_chips
+
+                    @pl.when((z_to > 0) | (x < owner_x))
+                    def _():
+                        forward_share(
+                            panel, x, z, sent_z, solved_sem.at[panel, x], at(z_to, x, core)
+                        )
+
+        def give_chunk(panel, mine, owner_x):
+            @pl.when(mine)
+            def _():
+                wait_bytes(solved.at[pl.ds(0, chunk - share)], solved_sem.at[panel, x])
+                for hop in (2, 1, 3):
+                    x_to = (x + hop) % X_CHIPS
+
+                    @pl.when((z > 0) | (x_to < owner_x))
+                    def _():
+                        forward(panel, x, sent_x, at(z, x_to, core))
+
+                forward(panel, x, sent_mate, mate)
+
+        def take_rest(panel, mine, owner_x):
+            for hop in range(1, X_CHIPS):
+                piece = (x + hop) % X_CHIPS
+                receive(panel, piece)
+
+                @pl.when(mine)
+                def _():
+                    forward(panel, piece, sent_mate, mate)
+
+            @pl.when(jnp.logical_not(mine))
+            def _():
+                receive(panel, x)
+
+            @pl.when(z > 0)
+            def _():
+                update(0, panel)
+
+        with_panel(0, give_share)
+        with_panel(1, give_chunk)
+
+        @pl.when(z > 0)
+        def _():
+            @pl.when(step < panels // 2)
+            def _():
+                relays(0, 2 * step, 2)
+
+            @pl.when(step == panels // 2)
+            def _():
+                send_near(1)
+
+            @pl.when((step >= panels - 2) & (step < panels))
+            def _():
+                relays(1, 2 * (step - (panels - 2)), 2)
+
+            @pl.when(step == 2)
+            def _():
+                take_samples(0)
+
+        with_panel(2, take_rest)
+        return carry
+
     @pl.when(in_chain)
     def _():
         wait_bytes(inverse, inverse_sem)
         take_samples(0)
-        lax.fori_loop(0, 2 * (2 * panels + CHUNKS - 2), chain_item, 0)
-        send_rows(0)
+        lax.fori_loop(0, 2 * (4 * x + CHUNKS + 2), chain_item, 0)
+
+    lax.fori_loop(0, panels + 2, spread_item, 0)
+    send_rows(0)
+
+    @pl.when(in_chain)
+    def _():
         relays(1, 0, panels)
 
-    def spread_item(step, carry):
-        @pl.when(step < panels)
-        def _():
-            panel = step
-
-            @pl.when(holds(panel, x))
-            def _():
-                receive(panel, x)
-                if z_chips == 8:
-                    @pl.when((z == 2) | (z == 6))
-                    def _():
-                        forward(panel, x, sent_z, at(z - 1, x, core))
-                        forward(panel, x, sent_z, at(z + 1, x, core))
-
-                        @pl.when((panel // 2) % 2 == z // 4)
-                        def _():
-                            forward(panel, x, sent_z, at(4, x, core))
-
-                for hop in (2, 1, 3):
-                    forward(panel, x, sent_x, at(z, (x + hop) % X_CHIPS, core))
-                forward(panel, x, sent_mate, mate)
-
-        @pl.when(step < panels // 2)
-        def _():
-            relays(0, 2 * step, 2)
-
-        @pl.when(step == panels // 2)
-        def _():
-            send_near(1)
-
-        @pl.when((step >= panels - 2) & (step < panels))
-        def _():
-            relays(1, 2 * (step - (panels - 2)), 2)
-
-        @pl.when(step == 1)
-        def _():
-            take_samples(0)
-
-        @pl.when(step >= 1)
-        def _():
-            panel = step - 1
-            for hop in range(1, X_CHIPS):
-                piece = (x + hop) % X_CHIPS
-
-                @pl.when(holds(panel, piece))
-                def _():
-                    receive(panel, piece)
-                    forward(panel, piece, sent_mate, mate)
-
-            for hop in range(X_CHIPS):
-                piece = (x + hop) % X_CHIPS
-
-                @pl.when(jnp.logical_not(holds(panel, piece)))
-                def _():
-                    receive(panel, piece)
-
-            update(0, panel)
-
-        return carry
-
     @pl.when(jnp.logical_not(in_chain))
     def _():
-        lax.fori_loop(0, panels + 1, spread_item, 0)
-        send_rows(0)
         relays(1, 4, panels - 4)
 
     take_samples(1)
@@ -334,20 +377,30 @@
 
         lax.fori_loop(0, me, sent, 0)
         wait_bytes(gathered.at[1, pl.ds(0, panels * 3 // n_samp)], sent_factor)
-        copies = 4 * (2 if z_chips == 8 else z_chips - 1)
-        wait_bytes(solved.at[pl.ds(0, copies * chunk)], sent_z)
+
+    def wait_rows(condition, rows, sem):
+        if rows > 0:
+            @pl.when(condition)
+            def _():
+                wait_bytes(solved.at[pl.ds(0, rows)], sem)
+
+    wait_rows(z > 0, 16 * chunk, sent_mate)
+    wait_rows(z > 0, 12 * chunk, sent_x)
+    wait_rows(z == 0, 4 * (z_chips - 1) * share, sent_z)
+    for place in range(X_CHIPS):
+        here = in_chain & (x == place)
+        wait_rows(here & (core == 0), 4 * (4 + place) * chunk, sent_mate)
+        wait_rows(here & (core == 1), 4 * (4 - place) * chunk, sent_mate)
+        wait_rows(here & (core == 1), 8 * (3 - place) * chunk, sent_chain)
+        wait_rows(here, (3 + place) * chunk, sent_x)
+        wait_rows(here, (4 * (z_chips - 1) + place) * share, sent_share)
+        others = (z_chips - 1) * (3 - place) + (z_chips - 2) * (place + 1)
+        wait_rows((z > 0) & (x == place), others * share, sent_z)
 
     @pl.when(jnp.logical_not(in_chain))
     def _():
         wait_bytes(gathered.at[:, pl.ds(0, panels * 3 // n_samp)], sent_factor)
 
-    if z_chips == 8:
-        @pl.when((z == 2) | (z == 6))
-        def _():
-            wait_bytes(solved.at[pl.ds(0, 10 * chunk)], sent_z)
-
-    wait_bytes(solved.at[pl.ds(0, 16 * chunk)], sent_mate)
-    wait_bytes(solved.at[pl.ds(0, 12 * chunk)], sent_x)
     wait_bytes(arrived.at[:, pl.ds(0, n_rows - 1)], sent_sample)
     wait_bytes(leaving.at[:, pl.ds(0, n_rows - 1)], sent_out)
     wait_bytes(landed, out_sem)
@@ -378,10 +431,11 @@
             pltpu.SemaphoreType.DMA((slots, panels)),
             pltpu.SemaphoreType.DMA((slots, panels)),
             pltpu.SemaphoreType.DMA((panels, CHUNKS)),
+            pltpu.SemaphoreType.DMA((panels,)),
             pltpu.SemaphoreType.DMA((slots,)),
             pltpu.SemaphoreType.DMA((panels,)),
         ]
-        + [pltpu.SemaphoreType.DMA] * 8,
+        + [pltpu.SemaphoreType.DMA] * 10,
         compiler_params=pltpu.CompilerParams(
             collective_id=0, has_side_effects=True, vmem_limit_bytes=60 * 2**20
         ),

time: 187 us -> 144 us (0.77)
  Pallas kernels: 184 us -> 141 us
    pallas_call x1, Pallas kernels: 184 us -> 141 us  [local(): pl.pallas_call(functools.partial(solve_kernel, n_rows, n_samp, panels), o...]
where the time goes in v3:
time: 144 us
  Pallas kernels  141 us (98%)
  other arithmetic  2.68 us (2%)
    pallas_call x1, Pallas kernels, local(): pl.pallas_call(functools.partial(solve_kernel, n_rows, n_samp, panels), o...  141 us

profile of v3, /device:TPU:1, one launch (start us, length us, event | category | flops | bytes accessed | tf_op | source)
XLA Modules:
  0.0 143.7 jit_solution(14131104632432753550)
XLA Ops:
  0.0 141.0 %shard_map.37 = bf16[2,8,32768]{2,1,0:T(8,128)(2,1)} custom-call(bf16[2,8,32768]{2,1,0:T(8,128)(2,1)} %bitcast.3, bf16[2,128,4096]{2,1,0:T(8,128)(2,1)} %factor_ref.1, bf16[2,512,512]{2,1,0:T(8,128)(2,1)} %inverse_ref.1), custom_call_target="tpu_custom_call" | custom-call | tf_op jit(solution)/shard_map/pallas_call | solution.py:416
  141.0 2.7 %convert_bitcast_fusion = f32[2,32768,8]{1,2,0:T(8,128)} fusion(bf16[2,8,32768]{2,1,0:T(8,128)(2,1)} %shard_map.37), kind=kLoop, calls=%fused_computation | loop fusion | flops 524288 | bytes 3145728 | tf_op jit(solution)/shard_map/transpose | solution.py:443

commit v4 on v3

--- a/solution.py
+++ b/solution.py
@@ -196,15 +196,15 @@
         wait_bytes(solved.at[place_of(panel, piece)], solved_sem.at[panel, piece])
 
     def chain_item(index, carry):
-        key = index // 2
-        piece = key % 2 + 2 * (index % 2)
-        panel = (key - piece + CHUNKS) // 2 - CHUNKS // 2
+        owner_x = x - (index // 2) % (x + 1)
+        piece = (index // 2) // (x + 1) - owner_x
+        panel = 2 * owner_x + index % 2
         rows = pl.ds(pl.multiple_of(piece * chunk, chunk), chunk)
 
-        @pl.when((panel >= 0) & (panel < 2 * x + 2))
+        @pl.when((piece >= 0) & (piece < CHUNKS) & (panel <= me))
         def _():
             place = place_of(panel, piece)
-            owner_x, owner_core = panel // 2, panel % 2
+            owner_core = panel % 2
 
             @pl.when(me == panel)
             def _():
@@ -347,7 +347,12 @@
     def _():
         wait_bytes(inverse, inverse_sem)
         take_samples(0)
-        lax.fori_loop(0, 2 * (4 * x + CHUNKS + 2), chain_item, 0)
+        lax.fori_loop(0, 2 * (x + CHUNKS) * (x + 1), chain_item, 0)
+
+        @pl.when(core == 0)
+        def _():
+            for piece in range(CHUNKS):
+                receive(me + 1, piece)
 
     lax.fori_loop(0, panels + 2, spread_item, 0)
     send_rows(0)

time: 144 us -> 133 us (0.924)
  Pallas kernels: 141 us -> 130 us
    pallas_call x1, Pallas kernels: 141 us -> 130 us  [local(): pl.pallas_call(functools.partial(solve_kernel, n_rows, n_samp, panels), o...]
where the time goes in v4:
time: 133 us; the launch traced here: 132 us
  Pallas kernels  130 us (98%)
  other arithmetic  2.68 us (2%)
    pallas_call x1, Pallas kernels, local(): pl.pallas_call(functools.partial(solve_kernel, n_rows, n_samp, panels), o...  130 us
    transpose x1, other arithmetic, local(): return result.astype(jnp.float32).transpose(0, 2, 1)  2.68 us

profile of v4, /device:TPU:1, one launch (start us, length us, event | category | flops | bytes accessed | tf_op | source)
XLA Modules:
  0.0 132.4 jit_solution(5604938153751779440)
XLA Ops:
  0.0 129.7 %shard_map.37 = bf16[2,8,32768]{2,1,0:T(8,128)(2,1)} custom-call(bf16[2,8,32768]{2,1,0:T(8,128)(2,1)} %bitcast.3, bf16[2,128,4096]{2,1,0:T(8,128)(2,1)} %factor_ref.1, bf16[2,512,512]{2,1,0:T(8,128)(2,1)} %inverse_ref.1), custom_call_target="tpu_custom_call" | custom-call | tf_op jit(solution)/shard_map/pallas_call | solution.py:421
  129.7 2.7 %convert_bitcast_fusion = f32[2,32768,8]{1,2,0:T(8,128)} fusion(bf16[2,8,32768]{2,1,0:T(8,128)(2,1)} %shard_map.37), kind=kLoop, calls=%fused_computation | loop fusion | flops 524288 | bytes 3145728 | tf_op jit(solution)/shard_map/transpose | solution.py:448

commit v5 on v4

--- a/solution.py
+++ b/solution.py
@@ -45,6 +45,8 @@
         return (z_to * X_CHIPS + x_to) * 2 + core_to
 
     mate = at(z, x, 1 - core)
+    ring = 2 * z_chips
+    group = x * ring + z * 2 + core
 
     def remote(source, target, send_sem, recv_sem, to_rows, to_samp):
         pltpu.make_async_remote_copy(
@@ -71,7 +73,7 @@
         return pl.ds(pl.multiple_of(index * block, block), block)
 
     def send_sample(slot, to):
-        source, target = sample_ref.at[slot, :, rows_of(to)], arrived.at[slot, me]
+        source, target = sample_ref.at[slot, :, rows_of(to)], arrived.at[slot, group]
 
         @pl.when(to != me)
         def _():
@@ -137,26 +139,47 @@
     def panel_rows(panel):
         return pl.ds(pl.multiple_of(panel * columns, columns), columns)
 
-    def update(slot, panel):
+    def take_factor(slot, panel):
         wait_bytes(part_of(slot, panel, (samp + 2) % n_samp), far_sem.at[slot, panel])
         wait_bytes(part_of(slot, panel, samp), own_sem.at[slot, panel])
+
+    def update(slot, panel):
+        take_factor(slot, panel)
         working[slot] -= dot_nt(solved[panel_rows(panel), :], gathered[slot, panel])
+
+    def updates(slot, start, count):
+        def body(step, carry):
+            update(slot, start + step)
+            return carry
+
+        lax.fori_loop(0, count, body, 0)
 
     def take_samples(slot):
         wait_bytes(arrived.at[slot], sample_sem.at[slot])
         working[slot] = arrived[slot].astype(jnp.float32).reshape(columns, block)
 
-    def send_rows(slot):
-        leaving[slot] = working[slot].reshape(n_rows, columns // n_rows, block).astype(jnp.bfloat16)
+    def send_rows(slot, piece):
+        rows = pl.ds(pl.multiple_of(piece * chunk, chunk), chunk)
+        value = working[slot, rows, :].reshape(ring, chunk // ring, block)
+        leaving[slot, pl.ds(piece * ring, ring)] = value.astype(jnp.bfloat16)
         target = landed.at[slot, :, rows_of(me)]
-        pltpu.make_async_copy(leaving.at[slot, me], target, out_sem).start()
 
         def body(step, carry):
-            to = (me + step) % n_rows
-            remote(leaving.at[slot, to], target, sent_out, out_sem, to, samp)
-            return carry
-
-        lax.fori_loop(1, n_rows, body, 0)
+            place = (2 * z + core + step) % ring
+            to = at(place // 2, piece, place % 2)
+            source = leaving.at[slot, piece * ring + place]
+
+            @pl.when(to != me)
+            def _():
+                remote(source, target, sent_out, out_sem, to, samp)
+
+            @pl.when(to == me)
+            def _():
+                pltpu.make_async_copy(source, target, out_sem).start()
+
+            return carry
+
+        lax.fori_loop(0, ring, body, 0)
 
     @pl.when(in_chain)
     def _():
@@ -168,17 +191,19 @@
     def _():
         send_near(0)
 
-    def send_rest(step, carry):
-        send_sample(0, plane + (me + step) % (n_rows - plane))
-        return carry
-
-    lax.fori_loop(0, n_rows - plane, send_rest, 0)
-
-    def send_second(step, carry):
-        send_sample(1, (me + step) % n_rows)
-        return carry
-
-    lax.fori_loop(0, n_rows, send_second, 0)
+    def send_rest():
+        def body(step, carry):
+            send_sample(0, plane + (me + step) % (n_rows - plane))
+            return carry
+
+        lax.fori_loop(0, n_rows - plane, body, 0)
+
+    def send_second():
+        def body(step, carry):
+            send_sample(1, (me + step) % n_rows)
+            return carry
+
+        lax.fori_loop(0, n_rows, body, 0)
 
     def place_of(panel, piece):
         return pl.ds(pl.multiple_of(panel * columns + piece * chunk, chunk), chunk)
@@ -266,9 +291,9 @@
 
         return carry
 
-    def spread_item(step, carry):
-        first = jnp.where(in_chain, 2 * x + 2, 0)
-
+    first = jnp.where(in_chain, 2 * x + 2, 0)
+
+    def parts(step):
         def with_panel(lag, body):
             panel = step - lag
 
@@ -315,33 +340,48 @@
             def _():
                 receive(panel, x)
 
-            @pl.when(z > 0)
-            def _():
-                update(0, panel)
-
+        return with_panel, give_share, give_chunk, take_rest
+
+    def spread_item(step, carry):
+        with_panel, give_share, give_chunk, take_rest = parts(step)
         with_panel(0, give_share)
         with_panel(1, give_chunk)
 
+        with_panel(2, take_rest)
+
         @pl.when(z > 0)
         def _():
-            @pl.when(step < panels // 2)
-            def _():
-                relays(0, 2 * step, 2)
-
-            @pl.when(step == panels // 2)
+            @pl.when(step < 2)
+            def _():
+                relays(0, panels // 2 * step, panels // 2)
+
+
+            @pl.when(step == 1)
             def _():
                 send_near(1)
 
-            @pl.when((step >= panels - 2) & (step < panels))
-            def _():
-                relays(1, 2 * (step - (panels - 2)), 2)
-
-            @pl.when(step == 2)
+
+            @pl.when(step == 4)
             def _():
                 take_samples(0)
-
-        with_panel(2, take_rest)
+                updates(0, 0, 3)
+
+            @pl.when(step > 4)
+            def _():
+                update(0, step - 2)
+
+            @pl.when(step == 5)
+            def _():
+                relays(1, 0, 2)
+
+            @pl.when(step > 5)
+            def _():
+                relays(1, 3 * step - 16, 3)
+
         return carry
+
+    send_rest()
+    send_second()
 
     @pl.when(in_chain)
     def _():
@@ -354,25 +394,59 @@
             for piece in range(CHUNKS):
                 receive(me + 1, piece)
 
-    lax.fori_loop(0, panels + 2, spread_item, 0)
-    send_rows(0)
+    lax.fori_loop(0, panels, spread_item, 0)
 
     @pl.when(in_chain)
     def _():
         relays(1, 0, panels)
 
-    @pl.when(jnp.logical_not(in_chain))
-    def _():
-        relays(1, 4, panels - 4)
-
+    last = panels - 1
+    early = panels - 3
+    with_panel, _, give_chunk, take_rest = parts(panels)
     take_samples(1)
 
-    def update_second(panel, carry):
-        update(1, panel)
+    @pl.when(z > 0)
+    def _():
+        updates(1, 0, early)
+
+    with_panel(1, give_chunk)
+    with_panel(2, take_rest)
+
+    @pl.when(z > 0)
+    def _():
+        update(0, last - 1)
+        take_factor(0, last)
+
+    @pl.when(z == 0)
+    def _():
+        updates(1, 0, early)
+
+    updates(1, early, last - early)
+    take_factor(1, last)
+
+    def finish(hop, carry):
+        piece = (x + hop) % X_CHIPS
+        rows = pl.ds(pl.multiple_of(piece * chunk, chunk), chunk)
+        mine = core == last % 2
+
+        @pl.when((first <= last) & jnp.logical_not(mine & (piece == x)))
+        def _():
+            receive(last, piece)
+
+        @pl.when((first <= last) & mine & (piece != x))
+        def _():
+            forward(last, piece, sent_mate, mate)
+
+        @pl.when(z > 0)
+        def _():
+            working[0, rows, :] -= dot_nt(solved[place_of(last, piece), :], gathered[0, last])
+
+        send_rows(0, piece)
+        working[1, rows, :] -= dot_nt(solved[place_of(last, piece), :], gathered[1, last])
+        send_rows(1, piece)
         return carry
 
-    lax.fori_loop(0, panels, update_second, 0)
-    send_rows(1)
+    lax.fori_loop(0, CHUNKS, finish, 0)
 
     @pl.when(in_chain)
     def _():

time: 133 us -> 129 us (0.970)
  Pallas kernels: 130 us -> 126 us
    pallas_call x1, Pallas kernels: 130 us -> 126 us  [local(): pl.pallas_call(functools.partial(solve_kernel, n_rows, n_samp, panels), o...]
where the time goes in v5:
time: 129 us
  Pallas kernels  126 us (98%)
  other arithmetic  2.68 us (2%)
    pallas_call x1, Pallas kernels, local(): pl.pallas_call(functools.partial(solve_kernel, n_rows, n_samp, panels), o...  126 us
    transpose x1, other arithmetic, local(): return result.astype(jnp.float32).transpose(0, 2, 1)  2.68 us

profile of v5, /device:TPU:1, one launch (start us, length us, event | category | flops | bytes accessed | tf_op | source)
XLA Modules:
  0.0 128.7 jit_solution(15249844923793178805)
XLA Ops:
  0.0 126.0 %shard_map.37 = bf16[2,8,32768]{2,1,0:T(8,128)(2,1)} custom-call(bf16[2,8,32768]{2,1,0:T(8,128)(2,1)} %bitcast.3, bf16[2,128,4096]{2,1,0:T(8,128)(2,1)} %factor_ref.1, bf16[2,512,512]{2,1,0:T(8,128)(2,1)} %inverse_ref.1), custom_call_target="tpu_custom_call" | custom-call | tf_op jit(solution)/shard_map/pallas_call | solution.py:495
  126.1 2.7 %convert_bitcast_fusion = f32[2,32768,8]{1,2,0:T(8,128)} fusion(bf16[2,8,32768]{2,1,0:T(8,128)(2,1)} %shard_map.37), kind=kLoop, calls=%fused_computation | loop fusion | flops 524288 | bytes 3145728 | tf_op jit(solution)/shard_map/transpose | solution.py:522

commit v6 on v5

--- a/solution.py
+++ b/solution.py
@@ -347,7 +347,7 @@
         with_panel(0, give_share)
         with_panel(1, give_chunk)
 
-        with_panel(2, take_rest)
+        with_panel(3, take_rest)
 
         @pl.when(z > 0)
         def _():
@@ -364,11 +364,11 @@
             @pl.when(step == 4)
             def _():
                 take_samples(0)
-                updates(0, 0, 3)
+                updates(0, 0, 2)
 
             @pl.when(step > 4)
             def _():
-                update(0, step - 2)
+                update(0, step - 3)
 
             @pl.when(step == 5)
             def _():
@@ -401,7 +401,7 @@
         relays(1, 0, panels)
 
     last = panels - 1
-    early = panels - 3
+    early = panels - 4
     with_panel, _, give_chunk, take_rest = parts(panels)
     take_samples(1)
 
@@ -410,10 +410,12 @@
         updates(1, 0, early)
 
     with_panel(1, give_chunk)
+    with_panel(3, take_rest)
     with_panel(2, take_rest)
 
     @pl.when(z > 0)
     def _():
+        update(0, last - 2)
         update(0, last - 1)
         take_factor(0, last)
 

time: 129 us -> 124 us (0.961)
  Pallas kernels: 126 us -> 121 us
    pallas_call x1, Pallas kernels: 126 us -> 121 us  [local(): pl.pallas_call(functools.partial(solve_kernel, n_rows, n_samp, panels), o...]
where the time goes in v6:
time: 124 us
  Pallas kernels  121 us (98%)
  other arithmetic  2.68 us (2%)
    pallas_call x1, Pallas kernels, local(): pl.pallas_call(functools.partial(solve_kernel, n_rows, n_samp, panels), o...  121 us
    transpose x1, other arithmetic, local(): return result.astype(jnp.float32).transpose(0, 2, 1)  2.68 us

profile of v6, /device:TPU:1, one launch (start us, length us, event | category | flops | bytes accessed | tf_op | source)
XLA Modules:
  0.0 123.6 jit_solution(14629148198533141069)
XLA Ops:
  0.0 120.9 %shard_map.37 = bf16[2,8,32768]{2,1,0:T(8,128)(2,1)} custom-call(bf16[2,8,32768]{2,1,0:T(8,128)(2,1)} %bitcast.3, bf16[2,128,4096]{2,1,0:T(8,128)(2,1)} %factor_ref.1, bf16[2,512,512]{2,1,0:T(8,128)(2,1)} %inverse_ref.1), custom_call_target="tpu_custom_call" | custom-call | tf_op jit(solution)/shard_map/pallas_call | solution.py:497
  120.9 2.7 %convert_bitcast_fusion = f32[2,32768,8]{1,2,0:T(8,128)} fusion(bf16[2,8,32768]{2,1,0:T(8,128)(2,1)} %shard_map.37), kind=kLoop, calls=%fused_computation | loop fusion | flops 524288 | bytes 3145728 | tf_op jit(solution)/shard_map/transpose | solution.py:524

commit v7 on v6

--- a/solution.py
+++ b/solution.py
@@ -253,7 +253,7 @@
 
             @pl.when((me == panel) & (core == 1))
             def _():
-                for ahead in (1, 3, 2):
+                for ahead in (1, 2, 3):
                     @pl.when(x + ahead < X_CHIPS)
                     def _():
                         forward(panel - 1, piece, sent_chain, at(z, x + ahead, 0))

time: 124 us -> 124 us (level)
  no operation moved by 1% of the time
where the time goes in v7:
time: 124 us
  Pallas kernels  121 us (98%)
  other arithmetic  2.68 us (2%)
    pallas_call x1, Pallas kernels, local(): pl.pallas_call(functools.partial(solve_kernel, n_rows, n_samp, panels), o...  121 us
    transpose x1, other arithmetic, local(): return result.astype(jnp.float32).transpose(0, 2, 1)  2.68 us

profile of v7, /device:TPU:1, one launch (start us, length us, event | category | flops | bytes accessed | tf_op | source)
XLA Modules:
  0.0 123.6 jit_solution(9385473071288984930)
XLA Ops:
  0.0 120.9 %shard_map.37 = bf16[2,8,32768]{2,1,0:T(8,128)(2,1)} custom-call(bf16[2,8,32768]{2,1,0:T(8,128)(2,1)} %bitcast.3, bf16[2,128,4096]{2,1,0:T(8,128)(2,1)} %factor_ref.1, bf16[2,512,512]{2,1,0:T(8,128)(2,1)} %inverse_ref.1), custom_call_target="tpu_custom_call" | custom-call | tf_op jit(solution)/shard_map/pallas_call | solution.py:497
  120.9 2.7 %convert_bitcast_fusion = f32[2,32768,8]{1,2,0:T(8,128)} fusion(bf16[2,8,32768]{2,1,0:T(8,128)(2,1)} %shard_map.37), kind=kLoop, calls=%fused_computation | loop fusion | flops 524288 | bytes 3145728 | tf_op jit(solution)/shard_map/transpose | solution.py:524
